TPU v7x, 1024 devices: a whole 4x4x32 slice. The times are simulated.
1024 devices in a mesh: ctx: 8 (over y, core), head: 16 (over z_lo), wide: 8 (over z_hi, x).
Axes of the slice: x: 4, y: 4, z: 32 (z_hi: 2, z_lo: 16; z = z_hi * 16 + z_lo), core: 2. Of those that a mesh axis runs over, the one named last changes fastest.
Arguments:
- query_rows: bfloat16 [8, 2048, 4096], P('wide', 'ctx', 'head'), may hold values from -105 to 105
- key_rows: bfloat16 [8, 2048, 4096], P('wide', 'ctx', 'head'), may hold values from -4.5 to 4.5
- value_rows: bfloat16 [8, 2048, 4096], P('wide', 'ctx', 'head'), may hold values from -6 to 6
- grad_out: bfloat16 [8, 2048, 4096], P('wide', 'ctx', 'head'), may hold values from -6 to 6
- segment: int32 [8, 2048], P('wide', 'ctx'), may hold values from 0 to 15, never falling along the last dimension, each value on 1 to 256 neighbouring positions
- frames: bfloat16 [8, 2048, 4096], P(None, 'ctx', 'wide'), may hold values from -6 to 6
Outputs:
- grad_query: bfloat16 [8, 2048, 4096], P('wide', 'ctx', 'head')
- grad_key: bfloat16 [8, 2048, 4096], P('wide', 'ctx', 'head')
- grad_value: bfloat16 [8, 2048, 4096], P('wide', 'ctx', 'head')
- grad_wq: float32 [8, 512, 4096], P('wide', 'ctx', 'head')
Inputs may be any that keep to these rules, and one draw needn't show every extreme that they name: Ids never fall along a recording; each segment spans 1 to 256 frames and one spans exactly 256.
All inputs are finite; a program needn't handle non-finite values.
Results may differ from a plain program's by a relative error of at most 0.01.
Values may be sent and summed in bfloat16 or wider, within the bound.
A program may use at most 32 MiB of HBM per device.

v0:
```python
import jax
import jax.numpy as jnp
from jax import lax
from jax.sharding import Mesh
from jax.sharding import PartitionSpec as P

HD = 128
WIDE = ("wide_0", "wide_1")


def shifted(value, axis, steps):
    count = lax.axis_size(axis)
    initial, last = (max(0, -steps), min(count, count - steps))
    return lax.ppermute(value, axis, [(source, source + steps) for source in range(initial, last)])


def laid_out(tiles, dim):
    tiles = jnp.moveaxis(tiles, 0, dim)
    dims = tiles.shape
    return tiles.reshape(*dims[:dim], dims[dim] * dims[dim + 1], *dims[dim + 2 :])


def all_blocks(value, axes, order):
    tiles = value[None]
    for k in order:
        tiles = lax.all_gather(tiles, axes[k], axis=0, tiled=True)
    block = [lax.axis_size(axes[k]) for k in reversed(order)]
    tiles = tiles.reshape(*block, *value.shape)
    turned = sorted(range(len(order)), key=lambda place: order[len(order) - 1 - place])
    return tiles.transpose(*turned, *range(len(order), tiles.ndim)).reshape(-1, *value.shape)


def gathered_by_axis(value, axes, order, dim):
    return laid_out(all_blocks(value, axes, order), dim)


def cut_along(value, dim, size):
    before, after = (value.shape[:dim], value.shape[dim + 1 :])
    return jnp.moveaxis(value.reshape(*before, size, -1, *after), dim, 0)


def sent_and_summed(value, axis, dim):
    tiles = cut_along(value, dim, lax.axis_size(axis))
    arrived = lax.all_to_all(tiles, axis, split_axis=0, concat_axis=0, tiled=True)
    return arrived.sum(axis=0)


def head_scores(left_heads, right_heads):
    return jnp.einsum("ihd,jhd->hij", left_heads, right_heads, preferred_element_type=jnp.float32)


def shards(query_rows, key_rows, value_rows, grad_out, segment, frames):
    length = query_rows.shape[1]
    columns = query_rows.shape[2]
    head_count = columns // HD
    factor = HD ** (-0.5)
    ctx_index = lax.axis_index("ctx")
    ctx_count = lax.axis_size("ctx")
    query_heads = query_rows.reshape(length, head_count, HD)
    key_heads = key_rows.reshape(length, head_count, HD)
    value_heads = value_rows.reshape(length, head_count, HD)
    grad_heads = grad_out.reshape(length, head_count, HD)
    own_segment = segment[0]
    prior_keys, prior_values, prior_segment = shifted((key_rows, value_rows, segment), "ctx", 1)
    prior_key_heads = prior_keys.reshape(length, head_count, HD)
    prior_value_heads = prior_values.reshape(length, head_count, HD)
    places = jnp.arange(length, dtype=jnp.int32)
    own_mask = (own_segment[:, None] == own_segment[None, :]) & (places[None, :] <= places[:, None])
    prior_mask = (own_segment[:, None] == prior_segment[0][None, :]) & (ctx_index > 0)
    own_scores = head_scores(query_heads, key_heads) * factor
    prior_scores = head_scores(query_heads, prior_key_heads) * factor
    row_max = jnp.maximum(
        jnp.max(jnp.where(own_mask, own_scores, -jnp.inf), axis=2, keepdims=True),
        jnp.max(jnp.where(prior_mask, prior_scores, -jnp.inf), axis=2, keepdims=True),
    )
    row_total = jnp.sum(
        jnp.where(own_mask, jnp.exp(own_scores - row_max), 0.0), axis=2, keepdims=True
    ) + jnp.sum(jnp.where(prior_mask, jnp.exp(prior_scores - row_max), 0.0), axis=2, keepdims=True)
    log_total = row_max + jnp.log(row_total)
    own_prob = jnp.where(own_mask, jnp.exp(own_scores - log_total), 0.0)
    prior_prob = jnp.where(prior_mask, jnp.exp(prior_scores - log_total), 0.0)
    own_grad_prob = head_scores(grad_heads, value_heads)
    prior_grad_prob = head_scores(grad_heads, prior_value_heads)
    row_delta = jnp.sum(own_prob * own_grad_prob, axis=2, keepdims=True) + jnp.sum(
        prior_prob * prior_grad_prob, axis=2, keepdims=True
    )
    own_grad_score = (own_prob * (own_grad_prob - row_delta)).astype(jnp.bfloat16)
    prior_grad_score = (prior_prob * (prior_grad_prob - row_delta)).astype(jnp.bfloat16)
    own_prob_low = own_prob.astype(jnp.bfloat16)
    grad_query_heads = (
        jnp.einsum("hij,jhd->ihd", own_grad_score, key_heads, preferred_element_type=jnp.float32)
        + jnp.einsum(
            "hij,jhd->ihd", prior_grad_score, prior_key_heads, preferred_element_type=jnp.float32
        )
    ) * factor
    grad_query = grad_query_heads.astype(jnp.bfloat16).reshape(1, length, columns)
    own_key_grad = jnp.einsum(
        "hij,ihd->jhd", own_grad_score, query_heads, preferred_element_type=jnp.float32
    )
    own_value_grad = jnp.einsum(
        "hij,ihd->jhd", own_prob_low, grad_heads, preferred_element_type=jnp.float32
    )
    later_queries, later_grads, later_segment = shifted((query_rows, grad_out, segment), "ctx", -1)
    later_log_total, later_delta = shifted((log_total, row_delta), "ctx", -1)
    later_query_heads = later_queries.reshape(length, head_count, HD)
    later_grad_heads = later_grads.reshape(length, head_count, HD)
    later_mask = (later_segment[0][:, None] == own_segment[None, :]) & (ctx_index < ctx_count - 1)
    cross_scores = head_scores(later_query_heads, key_heads) * factor
    cross_prob = jnp.where(later_mask, jnp.exp(cross_scores - later_log_total), 0.0)
    cross_grad_prob = head_scores(later_grad_heads, value_heads)
    cross_grad_score = (cross_prob * (cross_grad_prob - later_delta)).astype(jnp.bfloat16)
    later_key_grad = jnp.einsum(
        "hij,ihd->jhd", cross_grad_score, later_query_heads, preferred_element_type=jnp.float32
    )
    later_value_grad = jnp.einsum(
        "hij,ihd->jhd",
        cross_prob.astype(jnp.bfloat16),
        later_grad_heads,
        preferred_element_type=jnp.float32,
    )
    grad_key = (
        ((own_key_grad + later_key_grad) * factor).astype(jnp.bfloat16).reshape(1, length, columns)
    )
    grad_value = (
        (own_value_grad + later_value_grad).astype(jnp.bfloat16).reshape(1, length, columns)
    )
    width = frames.shape[2]
    row_block = width // ctx_count
    panel_sum = jnp.einsum(
        "rtd,rtc->dc",
        frames,
        gathered_by_axis(grad_query, WIDE, (0, 1), 0),
        preferred_element_type=jnp.float32,
    )
    grad_wq = sent_and_summed(panel_sum, "ctx", 0).reshape(1, row_block, columns)
    return (grad_query, grad_key, grad_value, grad_wq)


def solution(mesh):
    finer = Mesh(
        mesh.devices.reshape(mesh.shape["ctx"], mesh.shape["head"], 2, 4),
        ("ctx", "head", "wide_0", "wide_1"),
    )
    return jax.shard_map(
        shards,
        mesh=finer,
        in_specs=(
            P(WIDE, "ctx", "head"),
            P(WIDE, "ctx", "head"),
            P(WIDE, "ctx", "head"),
            P(WIDE, "ctx", "head"),
            P(WIDE, "ctx"),
            P(None, "ctx", WIDE),
        ),
        out_specs=(
            P(WIDE, "ctx", "head"),
            P(WIDE, "ctx", "head"),
            P(WIDE, "ctx", "head"),
            P(WIDE, "ctx", "head"),
        ),
        check_vma=False,
    )
```

profile of v0, /device:TPU:1, one launch (start us, length us, event | category | flops | bytes accessed | tf_op | source)
XLA Modules:
  0.0 151.5 jit_solution(3064963564954342231)
XLA Ops:
  7.2 16.2 %collective-permute-start.3 = (s32[1,256]{1,0:T(1,128)}, s32[1,256]{1,0:T(1,128)S(1)}, u32[]{:S(2)}, u32[]{:S(2)}) collective-permute-start(s32[1,256]{1,0:T(1,128)} %param.10), channel_id=1, source_target_pairs={{128,0},{256,128},{384,256},{512,384},{640,512},{768,640},{896,768... | collective-permute-start | bytes 3080 | tf_op jit(solution)/shard_map/ppermute | solution.py:14
  23.4 1.9 %collective-permute-start = (s32[1,256]{1,0:T(1,128)}, s32[1,256]{1,0:T(1,128)S(1)}, u32[]{:S(2)}, u32[]{:S(2)}) collective-permute-start(s32[1,256]{1,0:T(1,128)} %param.10), channel_id=1, source_target_pairs={{0,128},{128,256},{256,384},{384,512},{512,640},{640,768},{768,896... | collective-permute-start | bytes 3080 | tf_op jit(solution)/shard_map/ppermute | solution.py:14
  25.4 1.7 %copy.97 = bf16[1,256,256]{1,2,0:T(8,128)(2,1)} copy(bf16[1,256,256]{2,1,0:T(8,128)(2,1)} %param.7) | data formatting | bytes 262144 | tf_op args[1]
  27.0 1.9 %collective-permute-start.1 = (bf16[1,256,256]{1,2,0:T(8,128)(2,1)}, bf16[1,256,256]{1,2,0:T(8,128)(2,1)}, u32[]{:S(2)}, u32[]{:S(2)}) collective-permute-start(bf16[1,256,256]{1,2,0:T(8,128)(2,1)} %copy.97), channel_id=1, source_target_pairs={{0,128},{128,256},{256,384},{384,512},{512,640},{640,768},{768,896... | collective-permute-start | bytes 393224 | tf_op jit(solution)/shard_map/ppermute | solution.py:14
  29.0 1.7 %copy.102 = bf16[1,256,256]{1,2,0:T(8,128)(2,1)} copy(bf16[1,256,256]{2,1,0:T(8,128)(2,1)} %param.8) | data formatting | bytes 262144 | tf_op args[2]
  30.6 1.9 %collective-permute-start.2 = (bf16[1,256,256]{1,2,0:T(8,128)(2,1)}, bf16[1,256,256]{1,2,0:T(8,128)(2,1)}, u32[]{:S(2)}, u32[]{:S(2)}) collective-permute-start(bf16[1,256,256]{1,2,0:T(8,128)(2,1)} %copy.102), channel_id=1, source_target_pairs={{0,128},{128,256},{256,384},{384,512},{512,640},{640,768},{768,896... | collective-permute-start | bytes 393224 | tf_op jit(solution)/shard_map/ppermute | solution.py:14
  32.5 0.9 reshape.109
  33.5 1.1 copy.141
  34.8 0.9 reshape.106
  35.9 0.8 compare_and_fusion
  36.9 1.2 select_reduce_fusion.2
  38.4 1.3 multiply_reduce_fusion
  39.9 1.2 fusion.31
  41.1 1.2 fusion.7
  42.4 0.8 copy.122
  43.1 24.5 %all_gather.6 = bf16[2,1,256,256]{3,2,1,0:T(8,128)(2,1)} all-gather(bf16[1,1,256,256]{3,2,1,0:T(8,128)(2,1)} %copy.122), channel_id=1, replica_groups=mesh['ctx'=8,'head'=16,'wide_0'=2,'wide_1'=4] {'wide_0'}, dimensions={0}, use_global_device_ids=true | all-gather | bytes 393216 | tf_op jit(solution)/shard_map/all_gather | solution.py:26
  67.7 3.5 %collective-permute-start.4 = (bf16[1,256,256]{1,2,0:T(8,128)(2,1)S(1)}, bf16[1,256,256]{1,2,0:T(8,128)(2,1)}, u32[]{:S(2)}, u32[]{:S(2)}) collective-permute-start(bf16[1,256,256]{1,2,0:T(8,128)(2,1)S(1)} %copy-done.6), channel_id=1, source_target_pairs={{128,0},{256,128},{384,256},{512,384},{640,512},{768,640},{896,768... | collective-permute-start | bytes 393224 | tf_op jit(solution)/shard_map/ppermute | solution.py:14
  71.2 1.9 %collective-permute-start.6 = (bf16[1,256,256]{1,2,0:T(8,128)(2,1)S(1)}, bf16[1,256,256]{1,2,0:T(8,128)(2,1)}, u32[]{:S(2)}, u32[]{:S(2)}) collective-permute-start(bf16[1,256,256]{1,2,0:T(8,128)(2,1)S(1)} %copy.141), channel_id=1, source_target_pairs={{128,0},{256,128},{384,256},{512,384},{640,512},{768,640},{896,768... | collective-permute-start | bytes 393224 | tf_op jit(solution)/shard_map/ppermute | solution.py:14
  73.1 1.9 %collective-permute-start.5 = (f32[2,256,1]{1,0,2:T(2,128)S(1)}, f32[2,256,1]{1,0,2:T(2,128)S(1)}, u32[]{:S(2)}, u32[]{:S(2)}) collective-permute-start(f32[2,256,1]{1,0,2:T(2,128)S(1)} %bitcast.65), channel_id=1, source_target_pairs={{128,0},{256,128},{384,256},{512,384},{640,512},{768,640},{896,768... | collective-permute-start | bytes 6152 | tf_op jit(solution)/shard_map/ppermute | solution.py:14
  75.0 0.9 fusion.11
  76.0 0.9 fusion.38
  77.7 1.9 %collective-permute-start.7 = (f32[2,256,1]{1,0,2:T(2,128)S(1)}, f32[2,256,1]{1,0,2:T(2,128)S(1)}, u32[]{:S(2)}, u32[]{:S(2)}) collective-permute-start(f32[2,256,1]{1,0,2:T(2,128)S(1)} %bitcast.66), channel_id=1, source_target_pairs={{128,0},{256,128},{384,256},{512,384},{640,512},{768,640},{896,768... | collective-permute-start | bytes 6152 | tf_op jit(solution)/shard_map/ppermute | solution.py:14
  79.6 1.1 fusion.1
  80.7 42.6 %all-gather.2.cloned.1.call-done = bf16[8,1,256,256]{3,2,1,0:T(8,128)(2,1)} async-done(((bf16[2,1,256,256]{3,2,1,0:T(8,128)(2,1)}), bf16[8,1,256,256]{3,2,1,0:T(8,128)(2,1)}) %all-gather.2.cloned.1.call-update) | async-done | bytes 1048592 | tf_op jit(solution)/shard_map/all_gather | solution.py:26
  123.4 2.3 %copy.123 = bf16[4,2,1,256,256]{3,4,0,1,2:T(8,128)(2,1)} copy(bf16[4,2,1,256,256]{4,3,1,0,2:T(8,128)(2,1)} %bitcast.60) | data formatting | bytes 2097152 | tf_op jit(solution)/shard_map/reshape | solution.py:28
  125.7 2.0 %convolution_bitcast_fusion = f32[512,256]{0,1:T(8,128)S(1)} fusion(bf16[8,256,256]{1,2,0:T(8,128)(2,1)} %bitcast.61, bf16[8,256,512]{2,1,0:T(8,128)(2,1)S(1)} %copy-done), kind=kOutput, calls=%fused_computation.3 | convolution fusion | flops 536870912 | bytes 3670016 | tf_op jit(solution)/shard_map/rtd,rtc->dc/dot_general | solution.py:129
  127.6 1.0 copy.124
  128.6 5.9 %all-to-all-start = ((f32[8,64,256]{2,1,0:T(8,128)}), f32[8,64,256]{2,1,0:T(8,128)S(1)}, u32[]{:S(2)}, u32[]{:S(2)}) async-start(f32[8,64,256]{2,1,0:T(8,128)} %bitcast.54), calls=%async_computation | async-start | bytes 1048576 | tf_op jit(solution)/shard_map/all_to_all | solution.py:44
  134.5 1.5 fusion.8
  136.8 1.2 fusion.6
  138.0 0.8 copy.127
  138.8 5.2 %all-to-all-done = f32[8,64,256]{2,1,0:T(8,128)S(1)} async-done(((f32[8,64,256]{2,1,0:T(8,128)}), f32[8,64,256]{2,1,0:T(8,128)S(1)}, u32[]{:S(2)}, u32[]{:S(2)}) %all-to-all-start) | async-done | bytes 524320 | tf_op jit(solution)/shard_map/all_to_all | solution.py:44
  (45 shorter events, 3.2 us)
Async XLA Ops:
  7.2 118.5 %copy-start = (bf16[8,256,512]{2,1,0:T(8,128)(2,1)S(1)}, bf16[8,256,512]{2,1,0:T(8,128)(2,1)}, u32[]{:S(2)}) copy-start(bf16[8,256,512]{2,1,0:T(8,128)(2,1)} %param.11) | copy-start | bytes 6291460
  7.2 28.7 %copy-start.11 = (s32[1,256]{1,0:T(1,128)S(1)}, s32[1,256]{1,0:T(1,128)}, u32[]{:S(2)}) copy-start(s32[1,256]{1,0:T(1,128)} %param.10) | copy-start | bytes 3076
  7.2 28.5 %copy-start.10 = (bf16[1,256,256]{2,1,0:T(8,128)(2,1)S(1)}, bf16[1,256,256]{2,1,0:T(8,128)(2,1)}, u32[]{:S(2)}) copy-start(bf16[1,256,256]{2,1,0:T(8,128)(2,1)} %param.6) | copy-start | bytes 393220
  7.2 116.2 %all-gather.2.cloned.1.call-start = ((), (), s32[]{:S(2)}) async-start(), calls=%async_computation.1 | async-start | bytes 1310720 | tf_op jit(solution)/shard_map/all_gather | solution.py:26
  7.2 28.6 %collective-permute-start.3 = (s32[1,256]{1,0:T(1,128)}, s32[1,256]{1,0:T(1,128)S(1)}, u32[]{:S(2)}, u32[]{:S(2)}) collective-permute-start(s32[1,256]{1,0:T(1,128)} %param.10), channel_id=1, source_target_pairs={{128,0},{256,128},{384,256},{512,384},{640,512},{768,640},{896,768... | collective-permute-start | bytes 3080 | tf_op jit(solution)/shard_map/ppermute | solution.py:14
  23.4 12.4 %collective-permute-start = (s32[1,256]{1,0:T(1,128)}, s32[1,256]{1,0:T(1,128)S(1)}, u32[]{:S(2)}, u32[]{:S(2)}) collective-permute-start(s32[1,256]{1,0:T(1,128)} %param.10), channel_id=1, source_target_pairs={{0,128},{128,256},{256,384},{384,512},{512,640},{640,768},{768,896... | collective-permute-start | bytes 3080 | tf_op jit(solution)/shard_map/ppermute | solution.py:14
  27.0 9.9 %collective-permute-start.1 = (bf16[1,256,256]{1,2,0:T(8,128)(2,1)}, bf16[1,256,256]{1,2,0:T(8,128)(2,1)}, u32[]{:S(2)}, u32[]{:S(2)}) collective-permute-start(bf16[1,256,256]{1,2,0:T(8,128)(2,1)} %copy.97), channel_id=1, source_target_pairs={{0,128},{128,256},{256,384},{384,512},{512,640},{640,768},{768,896... | collective-permute-start | bytes 393224 | tf_op jit(solution)/shard_map/ppermute | solution.py:14
  30.6 7.8 %collective-permute-start.2 = (bf16[1,256,256]{1,2,0:T(8,128)(2,1)}, bf16[1,256,256]{1,2,0:T(8,128)(2,1)}, u32[]{:S(2)}, u32[]{:S(2)}) collective-permute-start(bf16[1,256,256]{1,2,0:T(8,128)(2,1)} %copy.102), channel_id=1, source_target_pairs={{0,128},{128,256},{256,384},{384,512},{512,640},{640,768},{768,896... | collective-permute-start | bytes 393224 | tf_op jit(solution)/shard_map/ppermute | solution.py:14
  33.5 3.2 %copy-start.7 = (bf16[256,2,128]{2,1,0:T(2,128)(2,1)}, bf16[256,2,128]{2,1,0:T(2,128)(2,1)S(1)}, u32[]{:S(2)}) copy-start(bf16[256,2,128]{2,1,0:T(2,128)(2,1)S(1)} %reshape.109) | copy-start | bytes 393220
  35.7 4.0 %copy-start.3 = (bf16[256,2,128]{2,1,0:T(2,128)(2,1)}, bf16[256,2,128]{2,1,0:T(2,128)(2,1)S(1)}, u32[]{:S(2)}) copy-start(bf16[256,2,128]{2,1,0:T(2,128)(2,1)S(1)} %reshape.106) | copy-start | bytes 393220
  35.8 3.9 %copy-start.5 = (bf16[1,256,256]{1,2,0:T(8,128)(2,1)}, bf16[1,256,256]{1,2,0:T(8,128)(2,1)S(1)}, u32[]{:S(2)}) copy-start(bf16[1,256,256]{1,2,0:T(8,128)(2,1)S(1)} %copy.140) | copy-start | bytes 393220
  36.7 3.1 %copy-start.1 = (pred[256,256]{0,1:T(8,128)(4,1)}, pred[256,256]{0,1:T(8,128)(4,1)S(1)}, u32[]{:S(2)}) copy-start(pred[256,256]{0,1:T(8,128)(4,1)S(1)} %get-tuple-element.26) | copy-start | bytes 196612
  39.9 27.7 %copy-start.6 = (bf16[1,256,256]{1,2,0:T(8,128)(2,1)S(1)}, bf16[1,256,256]{1,2,0:T(8,128)(2,1)}, u32[]{:S(2)}) copy-start(bf16[1,256,256]{1,2,0:T(8,128)(2,1)} %copy-done.5) | copy-start | bytes 393220
  39.9 35.1 %copy-start.2 = (pred[256,256]{0,1:T(8,128)(4,1)S(1)}, pred[256,256]{0,1:T(8,128)(4,1)}, u32[]{:S(2)}) copy-start(pred[256,256]{0,1:T(8,128)(4,1)} %copy-done.1) | copy-start | bytes 196612
  41.1 38.5 %copy-start.4 = (bf16[256,2,128]{2,1,0:T(2,128)(2,1)S(1)}, bf16[256,2,128]{2,1,0:T(2,128)(2,1)}, u32[]{:S(2)}) copy-start(bf16[256,2,128]{2,1,0:T(2,128)(2,1)} %copy-done.3) | copy-start | bytes 393220
  67.7 11.9 %collective-permute-start.4 = (bf16[1,256,256]{1,2,0:T(8,128)(2,1)S(1)}, bf16[1,256,256]{1,2,0:T(8,128)(2,1)}, u32[]{:S(2)}, u32[]{:S(2)}) collective-permute-start(bf16[1,256,256]{1,2,0:T(8,128)(2,1)S(1)} %copy-done.6), channel_id=1, source_target_pairs={{128,0},{256,128},{384,256},{512,384},{640,512},{768,640},{896,768... | collective-permute-start | bytes 393224 | tf_op jit(solution)/shard_map/ppermute | solution.py:14
  71.2 63.3 %collective-permute-start.6 = (bf16[1,256,256]{1,2,0:T(8,128)(2,1)S(1)}, bf16[1,256,256]{1,2,0:T(8,128)(2,1)}, u32[]{:S(2)}, u32[]{:S(2)}) collective-permute-start(bf16[1,256,256]{1,2,0:T(8,128)(2,1)S(1)} %copy.141), channel_id=1, source_target_pairs={{128,0},{256,128},{384,256},{512,384},{640,512},{768,640},{896,768... | collective-permute-start | bytes 393224 | tf_op jit(solution)/shard_map/ppermute | solution.py:14
  73.1 6.5 %collective-permute-start.5 = (f32[2,256,1]{1,0,2:T(2,128)S(1)}, f32[2,256,1]{1,0,2:T(2,128)S(1)}, u32[]{:S(2)}, u32[]{:S(2)}) collective-permute-start(f32[2,256,1]{1,0,2:T(2,128)S(1)} %bitcast.65), channel_id=1, source_target_pairs={{128,0},{256,128},{384,256},{512,384},{640,512},{768,640},{896,768... | collective-permute-start | bytes 6152 | tf_op jit(solution)/shard_map/ppermute | solution.py:14
  77.7 56.8 %collective-permute-start.7 = (f32[2,256,1]{1,0,2:T(2,128)S(1)}, f32[2,256,1]{1,0,2:T(2,128)S(1)}, u32[]{:S(2)}, u32[]{:S(2)}) collective-permute-start(f32[2,256,1]{1,0,2:T(2,128)S(1)} %bitcast.66), channel_id=1, source_target_pairs={{128,0},{256,128},{384,256},{512,384},{640,512},{768,640},{896,768... | collective-permute-start | bytes 6152 | tf_op jit(solution)/shard_map/ppermute | solution.py:14
  125.7 8.9 %copy-start.8 = (bf16[256,2,128]{2,1,0:T(2,128)(2,1)S(1)}, bf16[256,2,128]{2,1,0:T(2,128)(2,1)}, u32[]{:S(2)}) copy-start(bf16[256,2,128]{2,1,0:T(2,128)(2,1)} %copy-done.7) | copy-start | bytes 393220
  125.7 8.9 %copy-start.9 = (pred[256,256]{0,1:T(8,128)(4,1)S(1)}, pred[256,256]{0,1:T(8,128)(4,1)}, u32[]{:S(2)}) copy-start(pred[256,256]{0,1:T(8,128)(4,1)} %get-tuple-element.24) | copy-start | bytes 196612
  128.6 15.3 %all-to-all-start = ((f32[8,64,256]{2,1,0:T(8,128)}), f32[8,64,256]{2,1,0:T(8,128)S(1)}, u32[]{:S(2)}, u32[]{:S(2)}) async-start(f32[8,64,256]{2,1,0:T(8,128)} %bitcast.54), calls=%async_computation | async-start | bytes 1048576 | tf_op jit(solution)/shard_map/all_to_all | solution.py:44
Sparse Core Ops, SparseCore 0:
  67.8 55.5 all-gather.1
where the time goes:
time: 152 us; the launch traced here: 151 us
  waiting for transfers between devices  47.9 us (32%)
  starting transfers between devices  37.1 us (24%)
  blocking collectives  24.5 us (16%)
  between operations  14.4 us (9%)
  matrix products  13 us (9%)
  local copies, waits for them, and re-layouts  12.7 us (8%)
  other arithmetic  1.84 us (1%)
    all_gather x1, waiting for transfers between devices, all_blocks(): tiles = lax.all_gather(tiles, axes[k], axis=0, tiled=True)  42.6 us
    ppermute x8, starting transfers between devices, shifted(): lax.ppermute(value, axis, [(source, source + steps) for source in range(i...  31.2 us
    all_gather x1, blocking collectives, all_blocks(): tiles = lax.all_gather(tiles, axes[k], axis=0, tiled=True)  24.5 us
    all_to_all x1, starting transfers between devices, sent_and_summed(): lax.all_to_all(tiles, axis, split_axis=0, concat_axis=0, tiled=True)  5.86 us
    unnamed x29, local copies, waits for them, and re-layouts  5.67 us
    all_to_all x1, waiting for transfers between devices, sent_and_summed(): lax.all_to_all(tiles, axis, split_axis=0, concat_axis=0, tiled=True)  5.21 us
    dot_general x5, matrix products, head_scores(): jnp.einsum('ihd,jhd->hij', left_heads, right_heads, preferred_element_typ...  4.09 us
  transfers between devices with their start and end apart: 10, of which 2 were waited for; matrix products, arithmetic and copies ran while one was open for 15% of the time, Pallas kernels for 0%

commit v1 on v0

v1 whole, which is shorter than its diff:
```python
import functools

import jax
import jax.numpy as jnp
from jax import lax
from jax.experimental import pallas as pl
from jax.experimental.pallas import tpu as pltpu
from jax.sharding import PartitionSpec as P

HD = 128
MESH = pl.DeviceIdType.MESH
F32 = jnp.float32
BF16 = jnp.bfloat16
LOW = -1e30


def dot(a, b, dims):
    return lax.dot_general(a, b, (dims, ((), ())), preferred_element_type=F32)


def remote(src, dst, send, recv, where):
    return pltpu.make_async_remote_copy(
        src_ref=src, dst_ref=dst, send_sem=send, recv_sem=recv, device_id=where, device_id_type=MESH
    )


def kernel(
    nc, nx, heads, tok, width, parts,
    q_in, k_in, v_in, g_in, seg_in, fr_in,
    gq_out, gk_out, gv_out, wq_out,
    q, k, v, g, seg, bias, fl, ff, flt, fft, sc, dp, dsb, pb,
    lbuf, fbuf, acc, rs_s, rs_r, gqb, gkb, gvb, pks, pvs, pkr, pvr, wqb,
    in_sem, fl_sem, ff_sem, out_sem, kv_s, kv_r, pp_s, pp_r, z_s, z_r, xl_s, xl_r, xf_s, xf_r, c_s, c_r,
):
    c = lax.axis_index("ctx")
    w = lax.axis_index("wide")
    x = lax.rem(w, nx)
    half = w // nx
    part = tok // parts
    rows = width // nc
    factor = HD ** (-0.5)

    def ctx(step):
        return {"ctx": lax.rem(c + step, nc)}

    def across(step):
        return {"wide": half * nx + lax.rem(x + step, nx)}

    partner = {"wide": lax.rem(w + nx, 2 * nx)}

    barrier = pltpu.get_barrier_semaphore()
    others = [partner] + [across(j) for j in range(1, nx)] + [ctx(j) for j in range(1, nc)]
    for other in others:
        pl.semaphore_signal(barrier, inc=1, device_id=other, device_id_type=MESH)

    loads = []
    for h in range(heads):
        cols = pl.ds(h * HD, HD)
        loads.append(pltpu.make_async_copy(q_in.at[0, :, cols], q.at[h], in_sem.at[4 * h]))
        loads.append(pltpu.make_async_copy(k_in.at[0, :, cols], k.at[h, pl.ds(tok, tok)], in_sem.at[4 * h + 1]))
        loads.append(pltpu.make_async_copy(g_in.at[0, :, cols], g.at[h], in_sem.at[4 * h + 2]))
        loads.append(pltpu.make_async_copy(v_in.at[0, :, cols], v.at[h, pl.ds(tok, tok)], in_sem.at[4 * h + 3]))
    loads.append(pltpu.make_async_copy(seg_in, seg.at[1], in_sem.at[4 * heads]))
    own_frames = pltpu.make_async_copy(fr_in.at[pl.ds(half * nx, nx)], fl, fl_sem)
    far_frames = [
        pltpu.make_async_copy(
            fr_in.at[(1 - half) * nx + r, pl.ds(i * part, part)], ff.at[i, r], ff_sem.at[i * nx + r]
        )
        for i in range(parts)
        for r in range(nx)
    ]
    for copy in loads + [own_frames] + far_frames:
        copy.start()
    for copy in loads:
        copy.wait()

    for h in range(heads):
        sc[h, :, tok:] = dot(q[h], k[h, tok:], ((1,), (1,))) * factor
        dp[h, :, tok:] = dot(g[h], v[h, tok:], ((1,), (1,)))

    own_frames.wait()
    for r in range(nx):
        flt[r] = fl[r].T
    for copy in far_frames:
        copy.wait()
    for i in range(parts):
        fft[i] = ff[i].reshape(nx * part, width).T

    pl.semaphore_wait(barrier, len(others))

    seg_copy = remote(seg.at[1], seg.at[0], kv_s.at[2 * heads], kv_r.at[2 * heads], ctx(1))
    seg_copy.start()
    kv = []
    for h in range(heads):
        for n, ref in enumerate((k, v)):
            copy = remote(
                ref.at[h, pl.ds(tok, tok)], ref.at[h, pl.ds(0, tok)], kv_s.at[2 * h + n], kv_r.at[2 * h + n], ctx(1)
            )
            copy.start()
            kv.append(copy)

    mine = jnp.broadcast_to(seg[1], (HD, tok)).T[:, :1]
    query_place = lax.broadcasted_iota(jnp.int32, (tok, tok), 0)
    key_place = lax.broadcasted_iota(jnp.int32, (tok, tok), 1)
    bias[:, tok:] = jnp.where((mine == seg[1]) & (key_place <= query_place), 0.0, LOW)
    seg_copy.wait_recv()
    bias[:, :tok] = jnp.where((mine == seg[0]) & (c > 0), 0.0, LOW)

    z_copies = {}
    xl_copies = {}
    for h in range(heads):
        kv[2 * h].wait_recv()
        sc[h, :, :tok] = dot(q[h], k[h, :tok], ((1,), (1,))) * factor
        kv[2 * h + 1].wait_recv()
        dp[h, :, :tok] = dot(g[h], v[h, :tok], ((1,), (1,)))
        scores = sc[h] + bias[...]
        row_max = jnp.max(scores, axis=1, keepdims=True)
        weight = jnp.exp(scores - row_max)
        prob = weight * (1.0 / jnp.sum(weight, axis=1, keepdims=True))
        grad_prob = dp[h]
        row_delta = jnp.sum(prob * grad_prob, axis=1, keepdims=True)
        grad_score = (prob * (grad_prob - row_delta)).astype(BF16)
        dsb[h] = grad_score
        pb[h] = prob.astype(BF16)
        grad_query = (dot(grad_score, k[h], ((1,), (0,))) * factor).astype(BF16)
        lbuf[h, x] = grad_query
        gqb[:, h * HD : (h + 1) * HD] = grad_query
        for i in range(parts):
            copy = remote(
                lbuf.at[h, x, pl.ds(i * part, part)], fbuf.at[h, i, x], z_s.at[h * parts + i], z_r.at[h * parts + i],
                partner,
            )
            copy.start()
            z_copies[h, i] = copy
        for j in range(1, nx):
            copy = remote(lbuf.at[h, x], lbuf.at[h, x], xl_s.at[h * nx + j], xl_r.at[h * nx + j], across(j))
            copy.start()
            xl_copies[h, j] = copy

    outs = [pltpu.make_async_copy(gqb, gq_out.at[0], out_sem.at[0])]
    outs[0].start()

    for h in range(heads):
        cols = slice(h * HD, (h + 1) * HD)
        pks[:, cols] = dot(dsb[h, :, :tok], q[h], ((0,), (0,)))
        pvs[:, cols] = dot(pb[h, :, :tok], g[h], ((0,), (0,)))
    pp = [
        remote(pks, pkr, pp_s.at[0], pp_r.at[0], ctx(nc - 1)),
        remote(pvs, pvr, pp_s.at[1], pp_r.at[1], ctx(nc - 1)),
    ]
    for copy in pp:
        copy.start()

    for h in range(heads):
        for j in range(1, nx):
            xl_copies[h, j].wait_recv()
        total = dot(flt[0], lbuf[h, 0], ((1,), (0,)))
        for r in range(1, nx):
            total += dot(flt[r], lbuf[h, r], ((1,), (0,)))
        acc[h] = total

    own_key = []
    for h in range(heads):
        own_key.append((dot(dsb[h, :, tok:], q[h], ((0,), (0,))), dot(pb[h, :, tok:], g[h], ((0,), (0,)))))
    for copy in pp:
        copy.wait_recv()
    for h in range(heads):
        cols = slice(h * HD, (h + 1) * HD)
        gkb[:, cols] = ((own_key[h][0] + pkr[:, cols]) * factor).astype(BF16)
        gvb[:, cols] = (own_key[h][1] + pvr[:, cols]).astype(BF16)
    outs.append(pltpu.make_async_copy(gkb, gk_out.at[0], out_sem.at[1]))
    outs.append(pltpu.make_async_copy(gvb, gv_out.at[0], out_sem.at[2]))
    outs[1].start()
    outs[2].start()

    xf_copies = {}
    c_copies = {}
    order = [(h, i) for h in range(heads) for i in range(parts)]

    def pass_on(h, i):
        z_copies[h, i].wait_recv()
        for j in range(1, nx):
            n = (h * parts + i) * nx + j
            copy = remote(fbuf.at[h, i, x], fbuf.at[h, i, x], xf_s.at[n], xf_r.at[n], across(j))
            copy.start()
            xf_copies[h, i, j] = copy

    def add(h, i):
        for j in range(1, nx):
            xf_copies[h, i, j].wait_recv()
        total = acc[h] + dot(fft[i], fbuf[h, i].reshape(nx * part, HD), ((1,), (0,)))
        acc[h] = total
        if i == parts - 1:
            rs_s[h] = total.astype(BF16).reshape(nc, rows, HD)
            for j in range(1, nc):
                to = lax.rem(c + j, nc)
                copy = remote(rs_s.at[h, to], rs_r.at[h, j], c_s.at[h * nc + j], c_r.at[h * nc + j], ctx(j))
                copy.start()
                c_copies[h, j] = copy

    pass_on(*order[0])
    for n in range(1, len(order)):
        pass_on(*order[n])
        add(*order[n - 1])
    add(*order[-1])

    for h in range(heads):
        total = acc[h, pl.ds(pl.multiple_of(c * rows, rows), rows)]
        for j in range(1, nc):
            c_copies[h, j].wait_recv()
            total += rs_r[h, j].astype(F32)
        wqb[:, h * HD : (h + 1) * HD] = total
    outs.append(pltpu.make_async_copy(wqb, wq_out.at[0], out_sem.at[3]))
    outs[3].start()

    for copy in [seg_copy] + kv + pp:
        copy.wait_send()
    for group in (z_copies, xl_copies, xf_copies, c_copies):
        for copy in group.values():
            copy.wait_send()
    for copy in outs:
        copy.wait()


def solution(mesh):
    nc, nx = mesh.shape["ctx"], mesh.shape["wide"] // 2

    def shards(query_rows, key_rows, value_rows, grad_out, segment, frames):
        tok, columns = query_rows.shape[1:]
        heads = columns // HD
        width = frames.shape[2]
        parts = 4
        part = tok // parts
        rows = width // nc
        vm = pltpu.VMEM
        dma = pltpu.SemaphoreType.DMA
        return pl.pallas_call(
            functools.partial(kernel, nc, nx, heads, tok, width, parts),
            name="attention_grads",
            out_shape=[
                jax.ShapeDtypeStruct((1, tok, columns), BF16),
                jax.ShapeDtypeStruct((1, tok, columns), BF16),
                jax.ShapeDtypeStruct((1, tok, columns), BF16),
                jax.ShapeDtypeStruct((1, rows, columns), F32),
            ],
            in_specs=[pl.BlockSpec(memory_space=pltpu.HBM)] * 6,
            out_specs=[pl.BlockSpec(memory_space=pl.ANY)] * 4,
            scratch_shapes=[
                vm((heads, tok, HD), BF16),
                vm((heads, 2 * tok, HD), BF16),
                vm((heads, 2 * tok, HD), BF16),
                vm((heads, tok, HD), BF16),
                vm((2, 1, tok), jnp.int32),
                vm((tok, 2 * tok), F32),
                vm((nx, tok, width), BF16),
                vm((parts, nx, part, width), BF16),
                vm((nx, width, tok), BF16),
                vm((parts, width, nx * part), BF16),
                vm((heads, tok, 2 * tok), F32),
                vm((heads, tok, 2 * tok), F32),
                vm((heads, tok, 2 * tok), BF16),
                vm((heads, tok, 2 * tok), BF16),
                vm((heads, nx, tok, HD), BF16),
                vm((heads, parts, nx, part, HD), BF16),
                vm((heads, width, HD), F32),
                vm((heads, nc, rows, HD), BF16),
                vm((heads, nc, rows, HD), BF16),
                vm((tok, columns), BF16),
                vm((tok, columns), BF16),
                vm((tok, columns), BF16),
                vm((tok, columns), F32),
                vm((tok, columns), F32),
                vm((tok, columns), F32),
                vm((tok, columns), F32),
                vm((rows, columns), F32),
                dma((4 * heads + 1,)),
                dma,
                dma((parts * nx,)),
                dma((4,)),
                dma((2 * heads + 1,)),
                dma((2 * heads + 1,)),
                dma((2,)),
                dma((2,)),
                dma((heads * parts,)),
                dma((heads * parts,)),
                dma((heads * nx,)),
                dma((heads * nx,)),
                dma((heads * parts * nx,)),
                dma((heads * parts * nx,)),
                dma((heads * nc,)),
                dma((heads * nc,)),
            ],
            compiler_params=pltpu.CompilerParams(
                collective_id=0, has_side_effects=True, vmem_limit_bytes=40 * 1024 * 1024
            ),
        )(query_rows, key_rows, value_rows, grad_out, segment, frames)

    return jax.shard_map(
        shards,
        mesh=mesh,
        in_specs=(
            P("wide", "ctx", "head"),
            P("wide", "ctx", "head"),
            P("wide", "ctx", "head"),
            P("wide", "ctx", "head"),
            P("wide", "ctx"),
            P(None, "ctx", "wide"),
        ),
        out_specs=(
            P("wide", "ctx", "head"),
            P("wide", "ctx", "head"),
            P("wide", "ctx", "head"),
            P("wide", "ctx", "head"),
        ),
        check_vma=False,
    )
```

time: 152 us -> 83.7 us (0.55)
  the two profiles are of different devices: /device:TPU:1 before, /device:TPU:33 now
where the time goes in v1:
time: 83.7 us; the launch traced here: 83.4 us
  Pallas kernels  74.3 us (89%)
  local copies, waits for them, and re-layouts  8.47 us (10%)
    pallas_call x1, Pallas kernels, shards(): pl.pallas_call(functools.partial(kernel, nc, nx, heads, tok, width, parts...  74.3 us
    unnamed x16, local copies, waits for them, and re-layouts  8.47 us

profile of v1, /device:TPU:33, one launch (start us, length us, event | category | flops | bytes accessed | tf_op | source)
XLA Modules:
  0.0 83.4 jit_solution(16333334427217019023)
XLA Ops:
  0.6 0.0 copy-start
  0.6 1.6 %copy-done = bf16[8,256,512]{2,1,0:T(8,128)(2,1)S(1)} copy-done((bf16[8,256,512]{2,1,0:T(8,128)(2,1)S(1)}, bf16[8,256,512]{2,1,0:T(8,128)(2,1)}, u32[]{:S(2)}) %copy-start) | copy-done | bytes 2097176
  2.2 0.0 copy-start.1
  2.2 0.9 %copy-done.1 = bf16[1,256,256]{2,1,0:T(8,128)(2,1)S(1)} copy-done((bf16[1,256,256]{2,1,0:T(8,128)(2,1)S(1)}, bf16[1,256,256]{2,1,0:T(8,128)(2,1)}, u32[]{:S(2)}) %copy-start.1) | copy-done | bytes 131096
  3.1 0.0 copy-start.2
  3.1 0.9 %copy-done.2 = bf16[1,256,256]{2,1,0:T(8,128)(2,1)S(1)} copy-done((bf16[1,256,256]{2,1,0:T(8,128)(2,1)S(1)}, bf16[1,256,256]{2,1,0:T(8,128)(2,1)}, u32[]{:S(2)}) %copy-start.2) | copy-done | bytes 131096
  4.0 0.0 copy-start.3
  4.0 0.9 %copy-done.3 = bf16[1,256,256]{2,1,0:T(8,128)(2,1)S(1)} copy-done((bf16[1,256,256]{2,1,0:T(8,128)(2,1)S(1)}, bf16[1,256,256]{2,1,0:T(8,128)(2,1)}, u32[]{:S(2)}) %copy-start.3) | copy-done | bytes 131096
  4.9 0.0 copy-start.4
  4.9 0.9 %copy-done.4 = bf16[1,256,256]{2,1,0:T(8,128)(2,1)S(1)} copy-done((bf16[1,256,256]{2,1,0:T(8,128)(2,1)S(1)}, bf16[1,256,256]{2,1,0:T(8,128)(2,1)}, u32[]{:S(2)}) %copy-start.4) | copy-done | bytes 131096
  5.8 0.0 copy-start.5
  5.8 0.7 copy-done.5
  6.5 74.3 %attention_grads.1 = (bf16[1,256,256]{2,1,0:T(8,128)(2,1)S(1)}, bf16[1,256,256]{2,1,0:T(8,128)(2,1)S(1)}, bf16[1,256,256]{2,1,0:T(8,128)(2,1)S(1)}, f32[1,64,256]{2,1,0:T(8,128)S(1)}) custom-call(bf16[1,256,256]{2,1,0:T(8,128)(2,1)S(1)} %copy-done.1, bf16[1,256,256]{2,1,0:T(8,128)(2,1)S(1)} %copy-done.2, bf16[1,256,256]{2,1,0:T(8,128)(2,1)S(1)} %copy-done.3, ...), custom_call_target="tpu_custom_call" | custom-call | tf_op jit(solution)/shard_map/attention_grads/pallas_call | solution.py:237
  80.8 0.7 copy.14
  81.4 0.7 copy.15
  82.1 0.7 copy.16
  82.8 0.6 copy.17
Async XLA Ops:
  0.6 1.6 %copy-start = (bf16[8,256,512]{2,1,0:T(8,128)(2,1)S(1)}, bf16[8,256,512]{2,1,0:T(8,128)(2,1)}, u32[]{:S(2)}) copy-start(bf16[8,256,512]{2,1,0:T(8,128)(2,1)} %fr_in.1) | copy-start | bytes 6291460
  2.2 0.9 %copy-start.1 = (bf16[1,256,256]{2,1,0:T(8,128)(2,1)S(1)}, bf16[1,256,256]{2,1,0:T(8,128)(2,1)}, u32[]{:S(2)}) copy-start(bf16[1,256,256]{2,1,0:T(8,128)(2,1)} %q_in.1) | copy-start | bytes 393220
  3.1 0.9 %copy-start.2 = (bf16[1,256,256]{2,1,0:T(8,128)(2,1)S(1)}, bf16[1,256,256]{2,1,0:T(8,128)(2,1)}, u32[]{:S(2)}) copy-start(bf16[1,256,256]{2,1,0:T(8,128)(2,1)} %k_in.1) | copy-start | bytes 393220
  4.0 0.9 %copy-start.3 = (bf16[1,256,256]{2,1,0:T(8,128)(2,1)S(1)}, bf16[1,256,256]{2,1,0:T(8,128)(2,1)}, u32[]{:S(2)}) copy-start(bf16[1,256,256]{2,1,0:T(8,128)(2,1)} %v_in.1) | copy-start | bytes 393220
  4.9 0.9 %copy-start.4 = (bf16[1,256,256]{2,1,0:T(8,128)(2,1)S(1)}, bf16[1,256,256]{2,1,0:T(8,128)(2,1)}, u32[]{:S(2)}) copy-start(bf16[1,256,256]{2,1,0:T(8,128)(2,1)} %g_in.1) | copy-start | bytes 393220
  5.8 0.7 copy-start.5

commit v2 on v1

--- a/solution.py
+++ b/solution.py
@@ -25,19 +25,21 @@
 
 
 def kernel(
-    nc, nx, heads, tok, width, parts,
+    nc, nh, nx, heads, tok, width,
     q_in, k_in, v_in, g_in, seg_in, fr_in,
     gq_out, gk_out, gv_out, wq_out,
     q, k, v, g, seg, bias, fl, ff, flt, fft, sc, dp, dsb, pb,
-    lbuf, fbuf, acc, rs_s, rs_r, gqb, gkb, gvb, pks, pvs, pkr, pvr, wqb,
-    in_sem, fl_sem, ff_sem, out_sem, kv_s, kv_r, pp_s, pp_r, z_s, z_r, xl_s, xl_r, xf_s, xf_r, c_s, c_r,
+    lbuf, rbuf, fbuf, acc, rs_s, rs_r, pks, pvs, pkr, pvr,
+    in_sem, fl_sem, ff_sem, kv_s, kv_r, pp_s, pp_r, z_s, z_r, y_s, y_r, xl_s, xl_r, xf_s, xf_r, c_s, c_r,
 ):
     c = lax.axis_index("ctx")
     w = lax.axis_index("wide")
     x = lax.rem(w, nx)
     half = w // nx
-    part = tok // parts
+    part = tok // 2
     rows = width // nc
+    nz = 2 * nh
+    z = half * nh + lax.axis_index("head")
     factor = HD ** (-0.5)
 
     def ctx(step):
@@ -46,10 +48,12 @@
     def across(step):
         return {"wide": half * nx + lax.rem(x + step, nx)}
 
-    partner = {"wide": lax.rem(w + nx, 2 * nx)}
+    def along(way):
+        to = lax.rem(z + (1, -1)[way] * (nh // 2) + nz, nz)
+        return {"head": lax.rem(to, nh), "wide": to // nh * nx + x}
 
     barrier = pltpu.get_barrier_semaphore()
-    others = [partner] + [across(j) for j in range(1, nx)] + [ctx(j) for j in range(1, nc)]
+    others = [along(0), along(1)] + [across(j) for j in range(1, nx)] + [ctx(j) for j in range(1, nc)]
     for other in others:
         pl.semaphore_signal(barrier, inc=1, device_id=other, device_id_type=MESH)
 
@@ -66,7 +70,7 @@
         pltpu.make_async_copy(
             fr_in.at[(1 - half) * nx + r, pl.ds(i * part, part)], ff.at[i, r], ff_sem.at[i * nx + r]
         )
-        for i in range(parts)
+        for i in range(2)
         for r in range(nx)
     ]
     for copy in loads + [own_frames] + far_frames:
@@ -83,7 +87,7 @@
         flt[r] = fl[r].T
     for copy in far_frames:
         copy.wait()
-    for i in range(parts):
+    for i in range(2):
         fft[i] = ff[i].reshape(nx * part, width).T
 
     pl.semaphore_wait(barrier, len(others))
@@ -106,6 +110,7 @@
     seg_copy.wait_recv()
     bias[:, :tok] = jnp.where((mine == seg[0]) & (c > 0), 0.0, LOW)
 
+    y_copies = {}
     z_copies = {}
     xl_copies = {}
     for h in range(heads):
@@ -124,21 +129,17 @@
         pb[h] = prob.astype(BF16)
         grad_query = (dot(grad_score, k[h], ((1,), (0,))) * factor).astype(BF16)
         lbuf[h, x] = grad_query
-        gqb[:, h * HD : (h + 1) * HD] = grad_query
-        for i in range(parts):
+        gq_out[0, :, h * HD : (h + 1) * HD] = grad_query
+        for i in range(2):
             copy = remote(
-                lbuf.at[h, x, pl.ds(i * part, part)], fbuf.at[h, i, x], z_s.at[h * parts + i], z_r.at[h * parts + i],
-                partner,
+                lbuf.at[h, x, pl.ds(i * part, part)], rbuf.at[h, i], y_s.at[2 * h + i], y_r.at[2 * h + i], along(i)
             )
             copy.start()
-            z_copies[h, i] = copy
+            y_copies[h, i] = copy
         for j in range(1, nx):
             copy = remote(lbuf.at[h, x], lbuf.at[h, x], xl_s.at[h * nx + j], xl_r.at[h * nx + j], across(j))
             copy.start()
             xl_copies[h, j] = copy
-
-    outs = [pltpu.make_async_copy(gqb, gq_out.at[0], out_sem.at[0])]
-    outs[0].start()
 
     for h in range(heads):
         cols = slice(h * HD, (h + 1) * HD)
@@ -151,7 +152,14 @@
     for copy in pp:
         copy.start()
 
-    for h in range(heads):
+    def relay(h):
+        for i in range(2):
+            y_copies[h, i].wait_recv()
+            copy = remote(rbuf.at[h, i], fbuf.at[h, i, x], z_s.at[2 * h + i], z_r.at[2 * h + i], along(i))
+            copy.start()
+            z_copies[h, i] = copy
+
+    def near(h):
         for j in range(1, nx):
             xl_copies[h, j].wait_recv()
         total = dot(flt[0], lbuf[h, 0], ((1,), (0,)))
@@ -159,28 +167,28 @@
             total += dot(flt[r], lbuf[h, r], ((1,), (0,)))
         acc[h] = total
 
-    own_key = []
-    for h in range(heads):
-        own_key.append((dot(dsb[h, :, tok:], q[h], ((0,), (0,))), dot(pb[h, :, tok:], g[h], ((0,), (0,)))))
+    for h in range(heads):
+        relay(h)
+    for h in range(heads):
+        near(h)
+
     for copy in pp:
         copy.wait_recv()
     for h in range(heads):
         cols = slice(h * HD, (h + 1) * HD)
-        gkb[:, cols] = ((own_key[h][0] + pkr[:, cols]) * factor).astype(BF16)
-        gvb[:, cols] = (own_key[h][1] + pvr[:, cols]).astype(BF16)
-    outs.append(pltpu.make_async_copy(gkb, gk_out.at[0], out_sem.at[1]))
-    outs.append(pltpu.make_async_copy(gvb, gv_out.at[0], out_sem.at[2]))
-    outs[1].start()
-    outs[2].start()
+        own_key = dot(dsb[h, :, tok:], q[h], ((0,), (0,)))
+        own_value = dot(pb[h, :, tok:], g[h], ((0,), (0,)))
+        gk_out[0, :, cols] = ((own_key + pkr[:, cols]) * factor).astype(BF16)
+        gv_out[0, :, cols] = (own_value + pvr[:, cols]).astype(BF16)
 
     xf_copies = {}
     c_copies = {}
-    order = [(h, i) for h in range(heads) for i in range(parts)]
+    order = [(h, i) for h in range(heads) for i in range(2)]
 
     def pass_on(h, i):
         z_copies[h, i].wait_recv()
         for j in range(1, nx):
-            n = (h * parts + i) * nx + j
+            n = (2 * h + i) * nx + j
             copy = remote(fbuf.at[h, i, x], fbuf.at[h, i, x], xf_s.at[n], xf_r.at[n], across(j))
             copy.start()
             xf_copies[h, i, j] = copy
@@ -190,7 +198,7 @@
             xf_copies[h, i, j].wait_recv()
         total = acc[h] + dot(fft[i], fbuf[h, i].reshape(nx * part, HD), ((1,), (0,)))
         acc[h] = total
-        if i == parts - 1:
+        if i == 1:
             rs_s[h] = total.astype(BF16).reshape(nc, rows, HD)
             for j in range(1, nc):
                 to = lax.rem(c + j, nc)
@@ -209,42 +217,42 @@
         for j in range(1, nc):
             c_copies[h, j].wait_recv()
             total += rs_r[h, j].astype(F32)
-        wqb[:, h * HD : (h + 1) * HD] = total
-    outs.append(pltpu.make_async_copy(wqb, wq_out.at[0], out_sem.at[3]))
-    outs[3].start()
+        wq_out[0, :, h * HD : (h + 1) * HD] = total
 
     for copy in [seg_copy] + kv + pp:
         copy.wait_send()
-    for group in (z_copies, xl_copies, xf_copies, c_copies):
+    for group in (y_copies, z_copies, xl_copies, xf_copies, c_copies):
         for copy in group.values():
             copy.wait_send()
-    for copy in outs:
-        copy.wait()
+
+
+def store(*refs):
+    n = len(refs) // 2
+    for i in range(n):
+        pltpu.make_async_copy(refs[i], refs[n + i], refs[-1].at[i]).start()
+    for i in range(n):
+        pltpu.make_async_copy(refs[i], refs[n + i], refs[-1].at[i]).wait()
 
 
 def solution(mesh):
-    nc, nx = mesh.shape["ctx"], mesh.shape["wide"] // 2
+    nc, nh, nx = mesh.shape["ctx"], mesh.shape["head"], mesh.shape["wide"] // 2
 
     def shards(query_rows, key_rows, value_rows, grad_out, segment, frames):
         tok, columns = query_rows.shape[1:]
         heads = columns // HD
         width = frames.shape[2]
-        parts = 4
-        part = tok // parts
+        part = tok // 2
         rows = width // nc
         vm = pltpu.VMEM
         dma = pltpu.SemaphoreType.DMA
-        return pl.pallas_call(
-            functools.partial(kernel, nc, nx, heads, tok, width, parts),
+        shapes = [(1, tok, columns)] * 3 + [(1, rows, columns)]
+        types = [BF16] * 3 + [F32]
+        results = pl.pallas_call(
+            functools.partial(kernel, nc, nh, nx, heads, tok, width),
             name="attention_grads",
-            out_shape=[
-                jax.ShapeDtypeStruct((1, tok, columns), BF16),
-                jax.ShapeDtypeStruct((1, tok, columns), BF16),
-                jax.ShapeDtypeStruct((1, tok, columns), BF16),
-                jax.ShapeDtypeStruct((1, rows, columns), F32),
-            ],
-            in_specs=[pl.BlockSpec(memory_space=pltpu.HBM)] * 6,
-            out_specs=[pl.BlockSpec(memory_space=pl.ANY)] * 4,
+            out_shape=[vm(shape, kind) for shape, kind in zip(shapes, types)],
+            in_specs=[pl.BlockSpec(memory_space=pl.ANY)] * 6,
+            out_specs=[pl.BlockSpec(memory_space=vm)] * 4,
             scratch_shapes=[
                 vm((heads, tok, HD), BF16),
                 vm((heads, 2 * tok, HD), BF16),
@@ -253,47 +261,54 @@
                 vm((2, 1, tok), jnp.int32),
                 vm((tok, 2 * tok), F32),
                 vm((nx, tok, width), BF16),
-                vm((parts, nx, part, width), BF16),
+                vm((2, nx, part, width), BF16),
                 vm((nx, width, tok), BF16),
-                vm((parts, width, nx * part), BF16),
+                vm((2, width, nx * part), BF16),
                 vm((heads, tok, 2 * tok), F32),
                 vm((heads, tok, 2 * tok), F32),
                 vm((heads, tok, 2 * tok), BF16),
                 vm((heads, tok, 2 * tok), BF16),
                 vm((heads, nx, tok, HD), BF16),
-                vm((heads, parts, nx, part, HD), BF16),
+                vm((heads, 2, part, HD), BF16),
+                vm((heads, 2, nx, part, HD), BF16),
                 vm((heads, width, HD), F32),
                 vm((heads, nc, rows, HD), BF16),
                 vm((heads, nc, rows, HD), BF16),
-                vm((tok, columns), BF16),
-                vm((tok, columns), BF16),
-                vm((tok, columns), BF16),
                 vm((tok, columns), F32),
                 vm((tok, columns), F32),
                 vm((tok, columns), F32),
                 vm((tok, columns), F32),
-                vm((rows, columns), F32),
                 dma((4 * heads + 1,)),
                 dma,
-                dma((parts * nx,)),
-                dma((4,)),
+                dma((2 * nx,)),
                 dma((2 * heads + 1,)),
                 dma((2 * heads + 1,)),
                 dma((2,)),
                 dma((2,)),
-                dma((heads * parts,)),
-                dma((heads * parts,)),
+                dma((2 * heads,)),
+                dma((2 * heads,)),
+                dma((2 * heads,)),
+                dma((2 * heads,)),
                 dma((heads * nx,)),
                 dma((heads * nx,)),
-                dma((heads * parts * nx,)),
-                dma((heads * parts * nx,)),
+                dma((2 * heads * nx,)),
+                dma((2 * heads * nx,)),
                 dma((heads * nc,)),
                 dma((heads * nc,)),
             ],
             compiler_params=pltpu.CompilerParams(
-                collective_id=0, has_side_effects=True, vmem_limit_bytes=40 * 1024 * 1024
+                collective_id=0, has_side_effects=True, vmem_limit_bytes=60 * 1024 * 1024
             ),
         )(query_rows, key_rows, value_rows, grad_out, segment, frames)
+        return pl.pallas_call(
+            store,
+            name="store",
+            out_shape=[jax.ShapeDtypeStruct(shape, kind) for shape, kind in zip(shapes, types)],
+            in_specs=[pl.BlockSpec(memory_space=pl.ANY)] * 4,
+            out_specs=[pl.BlockSpec(memory_space=pl.ANY)] * 4,
+            scratch_shapes=[dma((4,))],
+            compiler_params=pltpu.CompilerParams(vmem_limit_bytes=1024 * 1024),
+        )(*results)
 
     return jax.shard_map(
         shards,

time: 83.7 us -> 71.3 us (0.85)
  the two profiles are of different devices: /device:TPU:33 before, /device:TPU:1 now
where the time goes in v2:
time: 71.3 us; the launch traced here: 71.1 us
  Pallas kernels  70.5 us (99%)
    pallas_call x1, Pallas kernels, shards(): pl.pallas_call(functools.partial(kernel, nc, nh, nx, heads, tok, width),...  69.7 us

profile of v2, /device:TPU:1, one launch (start us, length us, event | category | flops | bytes accessed | tf_op | source)
XLA Modules:
  0.0 71.1 jit_solution(1245225918167866163)
XLA Ops:
  0.6 69.7 %attention_grads.1 = (bf16[1,256,256]{2,1,0:T(8,128)(2,1)S(1)}, bf16[1,256,256]{2,1,0:T(8,128)(2,1)S(1)}, bf16[1,256,256]{2,1,0:T(8,128)(2,1)S(1)}, f32[1,64,256]{2,1,0:T(8,128)S(1)}) custom-call(bf16[1,256,256]{2,1,0:T(8,128)(2,1)} %q_in.1, bf16[1,256,256]{2,1,0:T(8,128)(2,1)} %k_in.1, bf16[1,256,256]{2,1,0:T(8,128)(2,1)} %v_in.1, ...), custom_call_target="tpu_custom_call" | custom-call | tf_op jit(solution)/shard_map/attention_grads/pallas_call | solution.py:250
  70.3 0.8 %store.1 = (bf16[1,256,256]{2,1,0:T(8,128)(2,1)}, bf16[1,256,256]{2,1,0:T(8,128)(2,1)}, bf16[1,256,256]{2,1,0:T(8,128)(2,1)}, f32[1,64,256]{2,1,0:T(8,128)}) custom-call(bf16[1,256,256]{2,1,0:T(8,128)(2,1)S(1)} %get-tuple-element.8.refs_0_, bf16[1,256,256]{2,1,0:T(8,128)(2,1)S(1)} %get-tuple-element.9.refs_1_, ...), custom_call_target="tpu_custom_call" | custom-call | tf_op jit(solution)/shard_map/store/pallas_call | solution.py:303

commit v3 on v2

v3 whole, which is shorter than its diff:
```python
import functools

import jax
import jax.numpy as jnp
from jax import lax
from jax.experimental import pallas as pl
from jax.experimental.pallas import tpu as pltpu
from jax.sharding import PartitionSpec as P

HD = 128
MESH = pl.DeviceIdType.MESH
F32 = jnp.float32
BF16 = jnp.bfloat16
LOW = -1e30


def dot(a, b, dims):
    return lax.dot_general(a, b, (dims, ((), ())), preferred_element_type=F32)


def remote(src, dst, send, recv, where):
    return pltpu.make_async_remote_copy(
        src_ref=src, dst_ref=dst, send_sem=send, recv_sem=recv, device_id=where, device_id_type=MESH
    )


def kernel(
    nc, nh, nx, hops, heads, tok, width,
    q_in, k_in, v_in, g_in, seg_in, fr_in,
    gq_out, gk_out, gv_out, wq_out,
    q, kv, g, seg, bias, fl, ff, flt, fft, sc, dp, dsb, pb,
    lbuf, rbuf, fbuf, acc, rs_s, rs_r, pks, pvs, pkr, pvr,
    in_sem, fl_sem, ff_sem, kv_s, kv_r, pp_s, pp_r, z_s, z_r, xl_s, xl_r, xf_s, xf_r, c_s, c_r,
):
    c = lax.axis_index("ctx")
    w = lax.axis_index("wide")
    x = lax.rem(w, nx)
    half = w // nx
    rows = width // nc
    nz = 2 * nh
    z = half * nh + lax.axis_index("head")
    part = tok // 2
    factor = HD ** (-0.5)

    def ctx(step):
        return {"ctx": lax.rem(c + step, nc)}

    def across(step):
        return {"wide": half * nx + lax.rem(x + step, nx)}

    def along(way):
        to = lax.rem(z + (1, -1)[way] * (nh // hops) + nz, nz)
        return {"head": lax.rem(to, nh), "wide": to // nh * nx + x}

    barrier = pltpu.get_barrier_semaphore()
    others = [along(0), along(1)] + [across(j) for j in range(1, nx)] + [ctx(j) for j in range(1, nc)]
    for other in others:
        pl.semaphore_signal(barrier, inc=1, device_id=other, device_id_type=MESH)

    loads = []
    for h in range(heads):
        cols = pl.ds(h * HD, HD)
        loads.append(pltpu.make_async_copy(q_in.at[0, :, cols], q.at[h], in_sem.at[4 * h]))
        loads.append(pltpu.make_async_copy(k_in.at[0, :, cols], kv.at[h, 0, pl.ds(tok, tok)], in_sem.at[4 * h + 1]))
        loads.append(pltpu.make_async_copy(g_in.at[0, :, cols], g.at[h], in_sem.at[4 * h + 2]))
        loads.append(pltpu.make_async_copy(v_in.at[0, :, cols], kv.at[h, 1, pl.ds(tok, tok)], in_sem.at[4 * h + 3]))
    loads.append(pltpu.make_async_copy(seg_in, seg.at[1], in_sem.at[4 * heads]))
    own_frames = pltpu.make_async_copy(fr_in.at[pl.ds(half * nx, nx)], fl, fl_sem)
    far_frames = pltpu.make_async_copy(fr_in.at[pl.ds((1 - half) * nx, nx)], ff, ff_sem)
    for copy in loads + [own_frames, far_frames]:
        copy.start()
    for copy in loads:
        copy.wait()

    @pl.when(c == 0)
    def _():
        seg[0] = jnp.zeros_like(seg[0])
        for h in range(heads):
            for n in range(2):
                kv[h, n, :tok] = jnp.zeros((tok, HD), BF16)

    @pl.when(c == nc - 1)
    def _():
        pkr[...] = jnp.zeros_like(pkr)
        pvr[...] = jnp.zeros_like(pvr)

    for h in range(heads):
        sc[h, :, tok:] = dot(q[h], kv[h, 0, tok:], ((1,), (1,))) * factor
        dp[h, :, tok:] = dot(g[h], kv[h, 1, tok:], ((1,), (1,)))


    pl.semaphore_wait(barrier, len(others))

    kv_copies = [
        remote(kv.at[h, :, pl.ds(tok, tok)], kv.at[h, :, pl.ds(0, tok)], kv_s.at[h], kv_r.at[h], ctx(1))
        for h in range(heads)
    ]
    seg_copy = remote(seg.at[1], seg.at[0], kv_s.at[heads], kv_r.at[heads], ctx(1))
    first = [seg_copy] + kv_copies
    has_prior, has_later = c > 0, c < nc - 1

    @pl.when(has_later)
    def _():
        for copy in first:
            copy.start()


    mine = jnp.broadcast_to(seg[1], (HD, tok)).T[:, :1]
    query_place = lax.broadcasted_iota(jnp.int32, (tok, tok), 0)
    key_place = lax.broadcasted_iota(jnp.int32, (tok, tok), 1)
    bias[:, tok:] = jnp.where((mine == seg[1]) & (key_place <= query_place), 0.0, LOW)
    pl.when(has_prior)(seg_copy.wait_recv)
    bias[:, :tok] = jnp.where((mine == seg[0]) & (c > 0), 0.0, LOW)

    z_copies = {}
    xl_copies = {}

    def hop(h, way, n, src):
        dst = fbuf.at[h, x, pl.ds(way * part, part)] if n == hops - 1 else rbuf.at[h, way, n]
        m = (2 * h + way) * hops + n
        copy = remote(src, dst, z_s.at[m], z_r.at[m], along(way))
        copy.start()
        z_copies[h, way, n] = copy

    for h in range(heads):
        pl.when(has_prior)(kv_copies[h].wait_recv)
        sc[h, :, :tok] = dot(q[h], kv[h, 0, :tok], ((1,), (1,))) * factor
        dp[h, :, :tok] = dot(g[h], kv[h, 1, :tok], ((1,), (1,)))
        scores = sc[h] + bias[...]
        row_max = jnp.max(scores, axis=1, keepdims=True)
        weight = jnp.exp(scores - row_max)
        prob = weight * (1.0 / jnp.sum(weight, axis=1, keepdims=True))
        grad_prob = dp[h]
        row_delta = jnp.sum(prob * grad_prob, axis=1, keepdims=True)
        grad_score = (prob * (grad_prob - row_delta)).astype(BF16)
        dsb[h] = grad_score
        pb[h] = prob.astype(BF16)
        grad_query = (dot(grad_score, kv[h, 0], ((1,), (0,))) * factor).astype(BF16)
        lbuf[h, x] = grad_query
        gq_out[0, :, h * HD : (h + 1) * HD] = grad_query
        for way in range(2):
            hop(h, way, 0, lbuf.at[h, x, pl.ds(way * part, part)])

    for h in range(heads):
        for j in range(1, nx):
            copy = remote(lbuf.at[h, x], lbuf.at[h, x], xl_s.at[h * nx + j], xl_r.at[h * nx + j], across(j))
            copy.start()
            xl_copies[h, j] = copy

    for h in range(heads):
        cols = slice(h * HD, (h + 1) * HD)
        pks[:, cols] = dot(dsb[h, :, :tok], q[h], ((0,), (0,)))
        pvs[:, cols] = dot(pb[h, :, :tok], g[h], ((0,), (0,)))
    pp = [
        remote(pks, pkr, pp_s.at[0], pp_r.at[0], ctx(nc - 1)),
        remote(pvs, pvr, pp_s.at[1], pp_r.at[1], ctx(nc - 1)),
    ]

    @pl.when(has_prior)
    def _():
        for copy in pp:
            copy.start()


    def near(h):
        for j in range(1, nx):
            xl_copies[h, j].wait_recv()
        total = dot(flt[0], lbuf[h, 0], ((1,), (0,)))
        for r in range(1, nx):
            total += dot(flt[r], lbuf[h, r], ((1,), (0,)))
        acc[h] = total

    own_frames.wait()
    for r in range(nx):
        flt[r] = fl[r].T
    far_frames.wait()
    for r in range(nx):
        fft[r] = ff[r].T

    for n in range(1, hops):
        for h in range(heads):
            for way in range(2):
                z_copies[h, way, n - 1].wait_recv()
                hop(h, way, n, rbuf.at[h, way, n - 1])
    for h in range(heads):
        near(h)

    @pl.when(has_later)
    def _():
        for copy in pp:
            copy.wait_recv()

    for h in range(heads):
        cols = slice(h * HD, (h + 1) * HD)
        own_key = dot(dsb[h, :, tok:], q[h], ((0,), (0,)))
        own_value = dot(pb[h, :, tok:], g[h], ((0,), (0,)))
        gk_out[0, :, cols] = ((own_key + pkr[:, cols]) * factor).astype(BF16)
        gv_out[0, :, cols] = (own_value + pvr[:, cols]).astype(BF16)

    xf_copies = {}
    c_copies = {}

    def pass_on(h):
        for way in range(2):
            z_copies[h, way, hops - 1].wait_recv()
        for j in range(1, nx):
            copy = remote(fbuf.at[h, x], fbuf.at[h, x], xf_s.at[h * nx + j], xf_r.at[h * nx + j], across(j))
            copy.start()
            xf_copies[h, j] = copy

    def add(h):
        for j in range(1, nx):
            xf_copies[h, j].wait_recv()
        total = acc[h]
        for r in range(nx):
            total += dot(fft[r], fbuf[h, r], ((1,), (0,)))
        acc[h] = total
        rs_s[:, :, h * HD : (h + 1) * HD] = total.astype(BF16).reshape(nc, rows, HD)

    for h in range(heads):
        pass_on(h)
    for h in range(heads):
        add(h)
    for j in range(1, nc):
        copy = remote(rs_s.at[lax.rem(c + j, nc)], rs_r.at[j], c_s.at[j], c_r.at[j], ctx(j))
        copy.start()
        c_copies[j] = copy
    own_rows = pl.ds(pl.multiple_of(c * rows, rows), rows)
    total = jnp.concatenate([acc[h, own_rows] for h in range(heads)], axis=1)
    for j in range(1, nc):
        c_copies[j].wait_recv()
        total += rs_r[j].astype(F32)
    wq_out[0] = total

    @pl.when(has_later)
    def _():
        for copy in first:
            copy.wait_send()

    @pl.when(has_prior)
    def _():
        for copy in pp:
            copy.wait_send()

    for group in (z_copies, xl_copies, xf_copies, c_copies):
        for copy in group.values():
            copy.wait_send()


def store(*refs):
    n = len(refs) // 2
    for i in range(n):
        pltpu.make_async_copy(refs[i], refs[n + i], refs[-1].at[i]).start()
    for i in range(n):
        pltpu.make_async_copy(refs[i], refs[n + i], refs[-1].at[i]).wait()


def solution(mesh):
    nc, nh, nx = mesh.shape["ctx"], mesh.shape["head"], mesh.shape["wide"] // 2

    def shards(query_rows, key_rows, value_rows, grad_out, segment, frames):
        tok, columns = query_rows.shape[1:]
        heads = columns // HD
        width = frames.shape[2]
        rows = width // nc
        vm = pltpu.VMEM
        dma = pltpu.SemaphoreType.DMA
        shapes = [(1, tok, columns)] * 3 + [(1, rows, columns)]
        types = [BF16] * 3 + [F32]
        results = pl.pallas_call(
            functools.partial(kernel, nc, nh, nx, 4, heads, tok, width),
            name="attention_grads",
            out_shape=[vm(shape, kind) for shape, kind in zip(shapes, types)],
            in_specs=[pl.BlockSpec(memory_space=pl.ANY)] * 6,
            out_specs=[pl.BlockSpec(memory_space=vm)] * 4,
            scratch_shapes=[
                vm((heads, tok, HD), BF16),
                vm((heads, 2, 2 * tok, HD), BF16),
                vm((heads, tok, HD), BF16),
                vm((2, 1, tok), jnp.int32),
                vm((tok, 2 * tok), F32),
                vm((nx, tok, width), BF16),
                vm((nx, tok, width), BF16),
                vm((nx, width, tok), BF16),
                vm((nx, width, tok), BF16),
                vm((heads, tok, 2 * tok), F32),
                vm((heads, tok, 2 * tok), F32),
                vm((heads, tok, 2 * tok), BF16),
                vm((heads, tok, 2 * tok), BF16),
                vm((heads, nx, tok, HD), BF16),
                vm((heads, 2, 3, tok // 2, HD), BF16),
                vm((heads, nx, tok, HD), BF16),
                vm((heads, width, HD), F32),
                vm((nc, rows, columns), BF16),
                vm((nc, rows, columns), BF16),
                vm((tok, columns), F32),
                vm((tok, columns), F32),
                vm((tok, columns), F32),
                vm((tok, columns), F32),
                dma((4 * heads + 1,)),
                dma,
                dma,
                dma((heads + 1,)),
                dma((heads + 1,)),
                dma((2,)),
                dma((2,)),
                dma((heads * 8,)),
                dma((heads * 8,)),
                dma((heads * nx,)),
                dma((heads * nx,)),
                dma((heads * nx,)),
                dma((heads * nx,)),
                dma((nc,)),
                dma((nc,)),
            ],
            compiler_params=pltpu.CompilerParams(
                collective_id=0, has_side_effects=True, vmem_limit_bytes=60 * 1024 * 1024
            ),
        )(query_rows, key_rows, value_rows, grad_out, segment, frames)
        return pl.pallas_call(
            store,
            name="store",
            out_shape=[jax.ShapeDtypeStruct(shape, kind) for shape, kind in zip(shapes, types)],
            in_specs=[pl.BlockSpec(memory_space=pl.ANY)] * 4,
            out_specs=[pl.BlockSpec(memory_space=pl.ANY)] * 4,
            scratch_shapes=[dma((4,))],
            compiler_params=pltpu.CompilerParams(vmem_limit_bytes=1024 * 1024),
        )(*results)

    return jax.shard_map(
        shards,
        mesh=mesh,
        in_specs=(
            P("wide", "ctx", "head"),
            P("wide", "ctx", "head"),
            P("wide", "ctx", "head"),
            P("wide", "ctx", "head"),
            P("wide", "ctx"),
            P(None, "ctx", "wide"),
        ),
        out_specs=(
            P("wide", "ctx", "head"),
            P("wide", "ctx", "head"),
            P("wide", "ctx", "head"),
            P("wide", "ctx", "head"),
        ),
        check_vma=False,
    )
```

time: 71.3 us -> 67.8 us (0.951)
  Pallas kernels: 70.5 us -> 67 us
    pallas_call x1, Pallas kernels: 69.7 us -> 66.2 us  [shards(): pl.pallas_call(functools.partial(kernel, nc, nh, nx, 4, heads, tok, width...]
where the time goes in v3:
time: 67.8 us; the launch traced here: 67.6 us
  Pallas kernels  67 us (99%)
    pallas_call x1, Pallas kernels, shards(): pl.pallas_call(functools.partial(kernel, nc, nh, nx, 4, heads, tok, width...  66.2 us

profile of v3, /device:TPU:1, one launch (start us, length us, event | category | flops | bytes accessed | tf_op | source)
XLA Modules:
  0.0 67.6 jit_solution(6082989426435257670)
XLA Ops:
  0.6 66.2 %attention_grads.1 = (bf16[1,256,256]{2,1,0:T(8,128)(2,1)S(1)}, bf16[1,256,256]{2,1,0:T(8,128)(2,1)S(1)}, bf16[1,256,256]{2,1,0:T(8,128)(2,1)S(1)}, f32[1,64,256]{2,1,0:T(8,128)S(1)}) custom-call(bf16[1,256,256]{2,1,0:T(8,128)(2,1)} %q_in.1, bf16[1,256,256]{2,1,0:T(8,128)(2,1)} %k_in.1, bf16[1,256,256]{2,1,0:T(8,128)(2,1)} %v_in.1, ...), custom_call_target="tpu_custom_call" | custom-call | tf_op jit(solution)/shard_map/attention_grads/pallas_call | solution.py:270
  66.8 0.8 %store.1 = (bf16[1,256,256]{2,1,0:T(8,128)(2,1)}, bf16[1,256,256]{2,1,0:T(8,128)(2,1)}, bf16[1,256,256]{2,1,0:T(8,128)(2,1)}, f32[1,64,256]{2,1,0:T(8,128)}) custom-call(bf16[1,256,256]{2,1,0:T(8,128)(2,1)S(1)} %get-tuple-element.8.refs_0_, bf16[1,256,256]{2,1,0:T(8,128)(2,1)S(1)} %get-tuple-element.9.refs_1_, ...), custom_call_target="tpu_custom_call" | custom-call | tf_op jit(solution)/shard_map/store/pallas_call | solution.py:320

commit v4 on v3

--- a/solution.py
+++ b/solution.py
@@ -141,11 +141,10 @@
         for way in range(2):
             hop(h, way, 0, lbuf.at[h, x, pl.ds(way * part, part)])
 
-    for h in range(heads):
-        for j in range(1, nx):
-            copy = remote(lbuf.at[h, x], lbuf.at[h, x], xl_s.at[h * nx + j], xl_r.at[h * nx + j], across(j))
-            copy.start()
-            xl_copies[h, j] = copy
+    for j in range(1, nx):
+        copy = remote(lbuf.at[:, x], lbuf.at[:, x], xl_s.at[j], xl_r.at[j], across(j))
+        copy.start()
+        xl_copies[j] = copy
 
     for h in range(heads):
         cols = slice(h * HD, (h + 1) * HD)
@@ -163,25 +162,32 @@
 
 
     def near(h):
-        for j in range(1, nx):
-            xl_copies[h, j].wait_recv()
         total = dot(flt[0], lbuf[h, 0], ((1,), (0,)))
         for r in range(1, nx):
             total += dot(flt[r], lbuf[h, r], ((1,), (0,)))
         acc[h] = total
 
-    own_frames.wait()
-    for r in range(nx):
-        flt[r] = fl[r].T
-    far_frames.wait()
-    for r in range(nx):
-        fft[r] = ff[r].T
-
-    for n in range(1, hops):
+    def relay(n):
         for h in range(heads):
             for way in range(2):
                 z_copies[h, way, n - 1].wait_recv()
                 hop(h, way, n, rbuf.at[h, way, n - 1])
+
+    relay(1)
+    own_frames.wait()
+    for r in range(nx):
+        flt[r] = fl[r].T
+    if hops > 2:
+        relay(2)
+    far_frames.wait()
+    for r in range(nx):
+        fft[r] = ff[r].T
+
+    for n in range(3, hops):
+        relay(n)
+
+    for j in range(1, nx):
+        xl_copies[j].wait_recv()
     for h in range(heads):
         near(h)
 
@@ -209,28 +215,30 @@
             xf_copies[h, j] = copy
 
     def add(h):
+        total = acc[h] + dot(fft[x], fbuf[h, x], ((1,), (0,)))
         for j in range(1, nx):
             xf_copies[h, j].wait_recv()
-        total = acc[h]
-        for r in range(nx):
+            r = lax.rem(x - j + nx, nx)
             total += dot(fft[r], fbuf[h, r], ((1,), (0,)))
         acc[h] = total
-        rs_s[:, :, h * HD : (h + 1) * HD] = total.astype(BF16).reshape(nc, rows, HD)
+        rs_s[h] = total.astype(BF16).reshape(nc, rows, HD)
+        for j in range(1, nc):
+            n = h * nc + j
+            copy = remote(rs_s.at[h, lax.rem(c + j, nc)], rs_r.at[h, j], c_s.at[n], c_r.at[n], ctx(j))
+            copy.start()
+            c_copies[h, j] = copy
 
     for h in range(heads):
         pass_on(h)
     for h in range(heads):
         add(h)
-    for j in range(1, nc):
-        copy = remote(rs_s.at[lax.rem(c + j, nc)], rs_r.at[j], c_s.at[j], c_r.at[j], ctx(j))
-        copy.start()
-        c_copies[j] = copy
     own_rows = pl.ds(pl.multiple_of(c * rows, rows), rows)
-    total = jnp.concatenate([acc[h, own_rows] for h in range(heads)], axis=1)
-    for j in range(1, nc):
-        c_copies[j].wait_recv()
-        total += rs_r[j].astype(F32)
-    wq_out[0] = total
+    for h in range(heads):
+        total = acc[h, own_rows]
+        for j in range(1, nc):
+            c_copies[h, j].wait_recv()
+            total += rs_r[h, j].astype(F32)
+        wq_out[0, :, h * HD : (h + 1) * HD] = total
 
     @pl.when(has_later)
     def _():
@@ -291,8 +299,8 @@
                 vm((heads, 2, 3, tok // 2, HD), BF16),
                 vm((heads, nx, tok, HD), BF16),
                 vm((heads, width, HD), F32),
-                vm((nc, rows, columns), BF16),
-                vm((nc, rows, columns), BF16),
+                vm((heads, nc, rows, HD), BF16),
+                vm((heads, nc, rows, HD), BF16),
                 vm((tok, columns), F32),
                 vm((tok, columns), F32),
                 vm((tok, columns), F32),
@@ -306,12 +314,12 @@
                 dma((2,)),
                 dma((heads * 8,)),
                 dma((heads * 8,)),
+                dma((nx,)),
+                dma((nx,)),
                 dma((heads * nx,)),
                 dma((heads * nx,)),
-                dma((heads * nx,)),
-                dma((heads * nx,)),
-                dma((nc,)),
-                dma((nc,)),
+                dma((heads * nc,)),
+                dma((heads * nc,)),
             ],
             compiler_params=pltpu.CompilerParams(
                 collective_id=0, has_side_effects=True, vmem_limit_bytes=60 * 1024 * 1024

time: 67.8 us -> 67.2 us (level)
  no operation moved by 1% of the time
where the time goes in v4:
time: 67.2 us; the launch traced here: 67 us
  Pallas kernels  66.4 us (99%)
    pallas_call x1, Pallas kernels, shards(): pl.pallas_call(functools.partial(kernel, nc, nh, nx, 4, heads, tok, width...  65.6 us

profile of v4, /device:TPU:1, one launch (start us, length us, event | category | flops | bytes accessed | tf_op | source)
XLA Modules:
  0.0 67.0 jit_solution(4221908986202762189)
XLA Ops:
  0.6 65.6 %attention_grads.1 = (bf16[1,256,256]{2,1,0:T(8,128)(2,1)S(1)}, bf16[1,256,256]{2,1,0:T(8,128)(2,1)S(1)}, bf16[1,256,256]{2,1,0:T(8,128)(2,1)S(1)}, f32[1,64,256]{2,1,0:T(8,128)S(1)}) custom-call(bf16[1,256,256]{2,1,0:T(8,128)(2,1)} %q_in.1, bf16[1,256,256]{2,1,0:T(8,128)(2,1)} %k_in.1, bf16[1,256,256]{2,1,0:T(8,128)(2,1)} %v_in.1, ...), custom_call_target="tpu_custom_call" | custom-call | tf_op jit(solution)/shard_map/attention_grads/pallas_call | solution.py:278
  66.2 0.8 %store.1 = (bf16[1,256,256]{2,1,0:T(8,128)(2,1)}, bf16[1,256,256]{2,1,0:T(8,128)(2,1)}, bf16[1,256,256]{2,1,0:T(8,128)(2,1)}, f32[1,64,256]{2,1,0:T(8,128)}) custom-call(bf16[1,256,256]{2,1,0:T(8,128)(2,1)S(1)} %get-tuple-element.8.refs_0_, bf16[1,256,256]{2,1,0:T(8,128)(2,1)S(1)} %get-tuple-element.9.refs_1_, ...), custom_call_target="tpu_custom_call" | custom-call | tf_op jit(solution)/shard_map/store/pallas_call | solution.py:328

commit v5 on v4

--- a/solution.py
+++ b/solution.py
@@ -232,6 +232,20 @@
         pass_on(h)
     for h in range(heads):
         add(h)
+    @pl.when(has_later)
+    def _():
+        for copy in first:
+            copy.wait_send()
+
+    @pl.when(has_prior)
+    def _():
+        for copy in pp:
+            copy.wait_send()
+
+    for group in (z_copies, xl_copies, xf_copies):
+        for copy in group.values():
+            copy.wait_send()
+
     own_rows = pl.ds(pl.multiple_of(c * rows, rows), rows)
     for h in range(heads):
         total = acc[h, own_rows]
@@ -239,20 +253,8 @@
             c_copies[h, j].wait_recv()
             total += rs_r[h, j].astype(F32)
         wq_out[0, :, h * HD : (h + 1) * HD] = total
-
-    @pl.when(has_later)
-    def _():
-        for copy in first:
-            copy.wait_send()
-
-    @pl.when(has_prior)
-    def _():
-        for copy in pp:
-            copy.wait_send()
-
-    for group in (z_copies, xl_copies, xf_copies, c_copies):
-        for copy in group.values():
-            copy.wait_send()
+    for copy in c_copies.values():
+        copy.wait_send()
 
 
 def store(*refs):

time: 67.2 us -> 67.1 us (level)
  no operation moved by 1% of the time
where the time goes in v5:
time: 67.1 us; the launch traced here: 67 us
  Pallas kernels  66.3 us (99%)
    pallas_call x1, Pallas kernels, shards(): pl.pallas_call(functools.partial(kernel, nc, nh, nx, 4, heads, tok, width...  65.5 us

profile of v5, /device:TPU:1, one launch (start us, length us, event | category | flops | bytes accessed | tf_op | source)
XLA Modules:
  0.0 67.0 jit_solution(18310743933684145198)
XLA Ops:
  0.6 65.5 %attention_grads.1 = (bf16[1,256,256]{2,1,0:T(8,128)(2,1)S(1)}, bf16[1,256,256]{2,1,0:T(8,128)(2,1)S(1)}, bf16[1,256,256]{2,1,0:T(8,128)(2,1)S(1)}, f32[1,64,256]{2,1,0:T(8,128)S(1)}) custom-call(bf16[1,256,256]{2,1,0:T(8,128)(2,1)} %q_in.1, bf16[1,256,256]{2,1,0:T(8,128)(2,1)} %k_in.1, bf16[1,256,256]{2,1,0:T(8,128)(2,1)} %v_in.1, ...), custom_call_target="tpu_custom_call" | custom-call | tf_op jit(solution)/shard_map/attention_grads/pallas_call | solution.py:280
  66.2 0.8 %store.1 = (bf16[1,256,256]{2,1,0:T(8,128)(2,1)}, bf16[1,256,256]{2,1,0:T(8,128)(2,1)}, bf16[1,256,256]{2,1,0:T(8,128)(2,1)}, f32[1,64,256]{2,1,0:T(8,128)}) custom-call(bf16[1,256,256]{2,1,0:T(8,128)(2,1)S(1)} %get-tuple-element.8.refs_0_, bf16[1,256,256]{2,1,0:T(8,128)(2,1)S(1)} %get-tuple-element.9.refs_1_, ...), custom_call_target="tpu_custom_call" | custom-call | tf_op jit(solution)/shard_map/store/pallas_call | solution.py:330
